TPU v7x, 32 devices: a whole 2x2x4 slice. The times are simulated.
32 devices in a mesh: group: 2 (over y), adapter: 4 (over z), tensor: 4 (over x, core).
Axes of the slice: x: 2, y: 2, z: 4, core: 2. Of those that a mesh axis runs over, the one named last changes fastest.
Arguments:
- queries: bfloat16 [1024, 8192], P(('group', 'adapter'), 'tensor'), parts along dimension 0, may hold values from -100 to 100
- cached_key_rows: bfloat16 [1024, 64, 1024], P(('group', 'adapter'), None, 'tensor'), parts along dimension 0, may hold values from -4 to 4
- cached_value_rows: bfloat16 [1024, 64, 1024], P(('group', 'adapter'), None, 'tensor'), parts along dimension 0, may hold values from -4 to 4
- cached_row_length: int32 [1024], P(('group', 'adapter')), parts along dimension 0, may hold values from 2 to 64, as said below
- row_adapter_index: int32 [1024, 1], P(('group', 'adapter')), parts along dimension 0, may hold values from 0 to 3; in each aligned block of 32 rows (0 to 31, 32 to 63, ...) at most 16 rows name the same one
- adapter_slot_index: int32 [8], P('group'), parts along dimension 0, may hold values from 0 to 3, each once
- output_weight: bfloat16 [8192, 8192], P('tensor', 'adapter'), may hold values from -0.0625 to 0.0625
- adapter_down_weight: bfloat16 [8, 8192, 64], P(('group', 'adapter'), 'tensor'), parts along dimension 0, may hold values from -0.0625 to 0.0625
- adapter_up_weight: bfloat16 [8, 64, 8192], P(('group', 'adapter')), parts along dimension 0, may hold values from -0.75 to 0.75
Outputs:
- projected: bfloat16 [1024, 8192], P(('group', 'adapter', 'tensor')), parts along dimension 0
There are 2 independent parts, one for each index of `group`. A program takes and returns all parts, laid end to end along the dimension named above; an argument that names none is the same for every part. Nothing has to cross between parts.
Inputs may be any that keep to these rules, and one draw needn't show every extreme that they name: `cached_row_length`: each row's number of cached positions; some row has all 64. `row_adapter_index`: within each aligned block of 32 rows no adapter is named more than 16 times, and in some block one adapter is named exactly 16 times. A permutation: adapter a is stored at entry adapter_slot_index[a] of adapter_down_weight and adapter_up_weight.
All inputs are finite; a program needn't handle non-finite values.
Results may differ from a plain program's by a relative error of at most 0.013.
Values may be sent and summed in bfloat16 or wider, within the bound.
A program may use at most 128 MiB of HBM per device.

v0:
```python
import jax
import jax.numpy as jnp
from jax import lax
from jax.sharding import PartitionSpec as P

HEAD_WIDTH = 128


def per_device(
    queries,
    cached_key_rows,
    cached_value_rows,
    cached_row_length,
    row_adapter_index,
    adapter_slot_index,
    output_weight,
    adapter_down_weight,
    adapter_up_weight,
):
    row_count = queries.shape[0]
    tensor_count = lax.axis_size("tensor")
    owner_count = lax.axis_size("adapter")
    quarter_rows = row_count // tensor_count
    capacity = max(2, 2 * quarter_rows // owner_count)
    context = cached_key_rows.shape[1]
    kv_local = cached_key_rows.shape[2] // HEAD_WIDTH
    query_heads = queries.reshape(row_count, kv_local, -1, HEAD_WIDTH)
    cached_keys = cached_key_rows.reshape(row_count, context, kv_local, HEAD_WIDTH)
    cached_values = cached_value_rows.reshape(row_count, context, kv_local, HEAD_WIDTH)
    logits = jnp.einsum(
        "rgsd,rcgd->rgsc", query_heads, cached_keys, preferred_element_type=jnp.float32
    ) * HEAD_WIDTH ** (-0.5)
    visible = (jnp.arange(context, dtype=jnp.int32)[None, :] < cached_row_length[:, None])[
        :, None, None, :
    ]
    logits = jnp.where(visible, logits, -1e30)
    highest = jnp.max(logits, axis=-1, keepdims=True)
    weights = jnp.exp(logits - highest)
    attention_probs = (weights / jnp.sum(weights, axis=-1, keepdims=True)).astype(jnp.bfloat16)
    attended = jnp.einsum(
        "rgsc,rcgd->rgsd", attention_probs, cached_values, preferred_element_type=jnp.float32
    )
    attended = attended.astype(jnp.bfloat16).reshape(row_count, -1)
    row_adapter = row_adapter_index[:, 0]
    adapter_count = adapter_slot_index.shape[0]
    matches = row_adapter[:, None] == jnp.arange(adapter_count, dtype=jnp.int32)[None, :]
    slot_index = jnp.sum(jnp.where(matches, adapter_slot_index[None, :], 0), axis=1)
    owner_hot = (slot_index[:, None] == jnp.arange(owner_count, dtype=jnp.int32)[None, :]).astype(
        jnp.int32
    )
    owner_hot = owner_hot.reshape(tensor_count, quarter_rows, owner_count)
    position = jnp.cumsum(owner_hot, axis=1) - 1
    placing = owner_hot[..., None] * (
        position[..., None] == jnp.arange(capacity, dtype=jnp.int32)
    ).astype(jnp.int32)
    split_heads = attended.reshape(tensor_count, quarter_rows, -1)
    send_rows = jnp.einsum(
        "qrjc,qrf->jqcf",
        placing.astype(jnp.bfloat16),
        split_heads,
        preferred_element_type=jnp.float32,
    ).astype(jnp.bfloat16)
    received_parts = lax.all_to_all(send_rows, "adapter", split_axis=0, concat_axis=0, tiled=True)
    rank_terms = jnp.einsum(
        "pato,ow->patw", received_parts, adapter_down_weight[0], preferred_element_type=jnp.float32
    )
    own_terms = lax.psum_scatter(rank_terms, "tensor", scatter_dimension=1, tiled=True)[:, 0]
    rank_activation = own_terms.astype(jnp.bfloat16)
    adapter_terms = jnp.einsum(
        "yhl,lq->yhq", rank_activation, adapter_up_weight[0], preferred_element_type=jnp.float32
    )
    panels = jnp.dot(
        lax.all_gather(attended, "adapter", axis=0, tiled=True),
        output_weight,
        preferred_element_type=jnp.float32,
    )
    shares = lax.psum_scatter(
        panels.reshape(owner_count, tensor_count, quarter_rows, -1),
        "tensor",
        scatter_dimension=1,
        tiled=True,
    )
    base_output_block, adapter_block = (
        lax.all_to_all(
            shares.reshape(owner_count, quarter_rows, -1),
            "adapter",
            split_axis=0,
            concat_axis=2,
            tiled=True,
        ),
        lax.all_to_all(adapter_terms, "adapter", split_axis=0, concat_axis=2, tiled=True),
    )
    base_output_rows = base_output_block[0]
    returned_result = adapter_block[0]
    model_width = base_output_rows.shape[1]
    gathered_terms = returned_result.reshape(capacity, owner_count, model_width)
    own_place = lax.dynamic_index_in_dim(
        placing, lax.axis_index("tensor"), 0, keepdims=False
    ).astype(jnp.float32)
    adapter_rows = jnp.einsum(
        "rjc,cjd->rd", own_place, gathered_terms, precision=lax.Precision.HIGHEST
    )
    return (base_output_rows + 2.0 * adapter_rows).astype(jnp.bfloat16)


def solution(mesh):
    return jax.shard_map(
        per_device,
        mesh=mesh,
        in_specs=(
            P(("group", "adapter"), "tensor"),
            P(("group", "adapter"), None, "tensor"),
            P(("group", "adapter"), None, "tensor"),
            P(("group", "adapter")),
            P(("group", "adapter"), None),
            P("group"),
            P("tensor", "adapter"),
            P(("group", "adapter"), "tensor", None),
            P(("group", "adapter"), None, None),
        ),
        out_specs=P(("group", "adapter", "tensor"), None),
        check_vma=False,
    )
```

profile of v0, /device:TPU:0, one launch (start us, length us, event | category | flops | bytes accessed | tf_op | source)
XLA Modules:
  0.0 256.8 jit_solution(6864575798373214465)
XLA Ops:
  6.5 0.0 copy-start
  6.5 0.0 all-gather.2.cloned.1.call-start
  6.5 1.2 copy.33
  7.8 0.7 iota_compare_fusion.2
  8.5 4.7 %fusion.39 = (f32[128,2,8]{2,1,0:T(2,128)S(1)}, f32[128,2,8,64]{3,2,1,0:T(8,128)S(1)}) fusion(bf16[128,2,8,128]{3,2,1,0:T(8,128)(2,1)S(1)} %bitcast.98, pred[128,64]{1,0:T(8,128)(4,1)S(1)} %iota_compare_fusion.2, bf16[128,64,256]{2,1,0:T(8,128)(2,1)} %param.10), kind=kOutput, calls=%fused_computation.44 | convolution fusion | flops 34078784 | bytes 5259264 | tf_op jit(solution)/shard_map/sub | solution.py:38
  13.2 0.0 copy-start.3
  13.3 0.0 copy-start.4
  13.3 3.5 %fusion.20 = bf16[128,2,8,128]{3,2,1,0:T(8,128)(2,1)S(1)} fusion(f32[128,2,8,64]{3,2,1,0:T(8,128)S(1)} %get-tuple-element.8, f32[128,2,8]{2,1,0:T(2,128)S(1)} %get-tuple-element.7, bf16[128,64,256]{2,1,0:T(8,128)(2,1)} %param.11), kind=kOutput, calls=%fused_computation.18 | convolution fusion | flops 34078720 | bytes 5251072 | tf_op jit(solution)/shard_map/rgsc,rcgd->rgsd/dot_general | solution.py:40
  16.7 0.9 copy.55
  17.7 0.0 all-gather.2.cloned.1.call-update
  17.7 0.0 all-reduce.4.cloned.1.call-start
  17.7 0.0 copy-done.3
  17.7 0.0 copy-done.4
  17.8 0.1 select_reduce_fusion
  17.8 0.1 eq.56
  17.9 48.6 %all-gather.2.cloned.1.call-done = bf16[512,2048]{1,0:T(8,128)(2,1)} async-done(((bf16[128,2048]{1,0:T(8,128)(2,1)}), bf16[512,2048]{1,0:T(8,128)(2,1)}) %all-gather.2.cloned.1.call-update) | async-done | bytes 2097168 | tf_op jit(solution)/shard_map/all_gather | solution.py:73
  66.5 10.5 %fusion.42 = f32[512,2048]{1,0:T(8,128)} fusion(bf16[512,2048]{1,0:T(8,128)(2,1)} %all-gather.2.cloned.1.call-done, bf16[2048,2048]{1,0:T(8,128)(2,1)} %param.15), kind=kOutput, calls=%fused_computation.45 | convolution fusion | flops 4294967296 | bytes 14680064 | tf_op jit(solution)/shard_map/dot_general | solution.py:72
  77.0 0.0 copy-start.5
  77.0 0.0 all-reduce.4.cloned.1.call-update
  77.0 0.1 fusion.30
  77.1 0.2 reshape.81
  77.3 0.1 copy.24
  77.4 0.1 reduce_window_sum.11
  77.5 0.0 copy-start.2
  77.5 0.1 copy.23
  77.6 0.7 fusion.28
  78.3 1.5 fusion.10
  79.8 3.5 %all-to-all-start.1 = ((bf16[4,4,16,2048]{3,2,1,0:T(8,128)(2,1)}), bf16[4,4,16,2048]{3,2,1,0:T(8,128)(2,1)S(1)}, u32[]{:S(2)}, u32[]{:S(2)}) async-start(bf16[4,4,16,2048]{3,2,1,0:T(8,128)(2,1)} %fusion.10), calls=%async_computation.1 | async-start | bytes 2097152 | tf_op jit(solution)/shard_map/all_to_all | solution.py:63
  83.3 0.0 copy-done.5
  83.3 0.6 dynamic-slice
  83.9 77.4 %all-reduce.4.cloned.1.call-done = f32[4,4,32,2048]{3,2,1,0:T(8,128)} async-done(((f32[4,4,32,2048]{3,2,1,0:T(8,128)}), f32[4,4,32,2048]{3,2,1,0:T(8,128)}) %all-reduce.4.cloned.1.call-update) | async-done | bytes 4194320
  161.4 3.0 %dynamic-slice_bitcast_fusion = f32[4,32,2048]{2,1,0:T(8,128)} fusion(f32[4,4,32,2048]{3,2,1,0:T(8,128)} %all-reduce.4.cloned.1.call-done, u32[]{:T(128)} %bitcast.25), kind=kLoop, calls=%fused_computation.19 | loop fusion | bytes 2097156 | tf_op jit(solution)/shard_map/reshape | solution.py:85
  164.3 0.0 all-to-all-done.1
  164.3 4.6 %all-to-all-start = ((f32[4,32,2048]{2,1,0:T(8,128)}), f32[4,32,2048]{2,1,0:T(8,128)S(1)}, u32[]{:S(2)}, u32[]{:S(2)}) async-start(f32[4,32,2048]{2,1,0:T(8,128)} %dynamic-slice_bitcast_fusion), calls=%async_computation | async-start | bytes 2097152 | tf_op jit(solution)/shard_map/all_to_all | solution.py:84
  168.9 0.0 copy-done.2
  168.9 0.4 fusion.26
  169.3 12.3 %all-reduce.1 = bf16[4,4,16,64]{3,2,1,0:T(8,128)(2,1)S(1)} all-reduce(f32[4,4,16,64]{3,2,1,0:T(8,128)S(1)} %fusion.26), channel_id=3, replica_groups=mesh['group'=2,'adapter'=4,'tensor'=4] {'tensor'}, use_global_device_ids=true, to_apply=%region_5.6.clone | all-reduce | flops 16384 | bytes 98304
  181.7 0.0 copy-done
  181.7 2.4 fusion.23
  184.1 10.4 %all-to-all-done = f32[4,32,2048]{2,1,0:T(8,128)S(1)} async-done(((f32[4,32,2048]{2,1,0:T(8,128)}), f32[4,32,2048]{2,1,0:T(8,128)S(1)}, u32[]{:S(2)}, u32[]{:S(2)}) %all-to-all-start) | async-done | bytes 1048608 | tf_op jit(solution)/shard_map/all_to_all | solution.py:84
  194.5 0.0 copy-start.1
  194.5 1.0 copy-done.1
  195.5 3.6 %all-to-all-start.2 = ((f32[4,16,8192]{2,1,0:T(8,128)}), f32[4,16,8192]{2,1,0:T(8,128)S(1)}, u32[]{:S(2)}, u32[]{:S(2)}) async-start(f32[4,16,8192]{2,1,0:T(8,128)} %fusion.23), calls=%async_computation.2 | async-start | bytes 4194304 | tf_op jit(solution)/shard_map/all_to_all | solution.py:91
  199.1 1.9 copy.22
  201.0 1.6 copy.35
  202.6 44.1 %all-to-all-done.2 = f32[4,16,8192]{2,1,0:T(8,128)S(1)} async-done(((f32[4,16,8192]{2,1,0:T(8,128)}), f32[4,16,8192]{2,1,0:T(8,128)S(1)}, u32[]{:S(2)}, u32[]{:S(2)}) %all-to-all-start.2) | async-done | bytes 2097184 | tf_op jit(solution)/shard_map/all_to_all | solution.py:91
  246.8 3.2 %fusion.3 = bf16[32,8192]{1,0:T(8,128)(2,1)} fusion(f32[32,8192]{1,0:T(8,128)} %bitcast.94, f32[4,16,8192]{2,1,0:T(8,128)S(1)} %all-to-all-done.2, s32[4,32,4,16]{1,3,2,0:T(8,128)} %get-tuple-element.5, s32[]{:T(128)S(6)} %select_n.14), kind=kOutput, calls=%fused_computation.4 | convolution fusion | flops 202115072 | bytes 3702788 | tf_op jit(solution)/shard_map/rjc,cjd->rd/dot_general | solution.py:100
  (1 shorter events, 0.0 us)
Async XLA Ops:
  6.5 175.1 %copy-start = (bf16[1,64,8192]{2,1,0:T(8,128)(2,1)S(1)}, bf16[1,64,8192]{2,1,0:T(8,128)(2,1)}, u32[]{:S(2)}) copy-start(bf16[1,64,8192]{2,1,0:T(8,128)(2,1)} %param.17) | copy-start | bytes 3145732
  6.5 59.9 %all-gather.2.cloned.1.call-start = ((), (), s32[]{:S(2)}) async-start(), calls=%async_computation.3 | async-start | bytes 2621440 | tf_op jit(solution)/shard_map/all_gather | solution.py:73
  13.2 4.5 %copy-start.3 = (s32[4]{0:T(128)S(1)}, s32[4]{0:T(128)}, u32[]{:S(2)}) copy-start(s32[4]{0:T(128)} %param.14) | copy-start | bytes 52
  13.3 4.5 %copy-start.4 = (s32[128,1]{0,1:T(1,128)S(1)}, s32[128,1]{0,1:T(1,128)}, u32[]{:S(2)}) copy-start(s32[128,1]{0,1:T(1,128)} %param.13) | copy-start | bytes 1540
  17.7 143.7 %all-reduce.4.cloned.1.call-start = ((), (), s32[]{:S(2)}) async-start(), calls=%async_computation.4 | async-start | bytes 8388608
  77.0 6.4 %copy-start.5 = (u32[32]{0:T(128)S(1)}, u32[32]{0:T(128)}, u32[]{:S(2)}) copy-start(u32[32]{0:T(128)} %constant.32) | copy-start | bytes 388
  77.5 91.4 %copy-start.2 = (bf16[1,2048,64]{1,2,0:T(8,128)(2,1)S(1)}, bf16[1,2048,64]{1,2,0:T(8,128)(2,1)}, u32[]{:S(2)}) copy-start(bf16[1,2048,64]{1,2,0:T(8,128)(2,1)} %param.16) | copy-start | bytes 786436
  79.8 84.5 %all-to-all-start.1 = ((bf16[4,4,16,2048]{3,2,1,0:T(8,128)(2,1)}), bf16[4,4,16,2048]{3,2,1,0:T(8,128)(2,1)S(1)}, u32[]{:S(2)}, u32[]{:S(2)}) async-start(bf16[4,4,16,2048]{3,2,1,0:T(8,128)(2,1)} %fusion.10), calls=%async_computation.1 | async-start | bytes 2097152 | tf_op jit(solution)/shard_map/all_to_all | solution.py:63
  164.3 30.2 %all-to-all-start = ((f32[4,32,2048]{2,1,0:T(8,128)}), f32[4,32,2048]{2,1,0:T(8,128)S(1)}, u32[]{:S(2)}, u32[]{:S(2)}) async-start(f32[4,32,2048]{2,1,0:T(8,128)} %dynamic-slice_bitcast_fusion), calls=%async_computation | async-start | bytes 2097152 | tf_op jit(solution)/shard_map/all_to_all | solution.py:84
  194.5 1.0 copy-start.1
  195.5 51.3 %all-to-all-start.2 = ((f32[4,16,8192]{2,1,0:T(8,128)}), f32[4,16,8192]{2,1,0:T(8,128)S(1)}, u32[]{:S(2)}, u32[]{:S(2)}) async-start(f32[4,16,8192]{2,1,0:T(8,128)} %fusion.23), calls=%async_computation.2 | async-start | bytes 4194304 | tf_op jit(solution)/shard_map/all_to_all | solution.py:91
Sparse Core Ops, SparseCore 0:
  17.8 48.6 all-gather.1
  77.1 84.1 all-reduce.3
where the time goes:
time: 257 us
  waiting for transfers between devices  181 us (70%)
  matrix products  26.1 us (10%)
  between operations  13.6 us (5%)
  blocking collectives  12.3 us (5%)
  starting transfers between devices  11.8 us (5%)
  local copies, waits for them, and re-layouts  10.7 us (4%)
    unnamed x3, waiting for transfers between devices  77.5 us
    all_gather x1, waiting for transfers between devices, per_device(): lax.all_gather(attended, 'adapter', axis=0, tiled=True)  48.6 us
    all_to_all x1, waiting for transfers between devices, per_device(): lax.all_to_all(adapter_terms, 'adapter', split_axis=0, concat_axis=2, til...  44.1 us
    unnamed x1, blocking collectives  12.3 us
    dot_general x1, matrix products, per_device(): jnp.dot(lax.all_gather(attended, 'adapter', axis=0, tiled=True), output_w...  10.5 us
    all_to_all x1, waiting for transfers between devices, per_device(): lax.all_to_all(shares.reshape(owner_count, quarter_rows, -1), 'adapter',...  10.4 us
    unnamed x16, local copies, waits for them, and re-layouts  5.39 us
  transfers between devices with their start and end apart: 5, of which 4 were waited for; matrix products, arithmetic and copies ran while one was open for 5% of the time, Pallas kernels for 0%

commit v1 on v0

--- a/solution.py
+++ b/solution.py
@@ -1,9 +1,474 @@
+import functools
+
 import jax
 import jax.numpy as jnp
 from jax import lax
+from jax.experimental import pallas as pl
+from jax.experimental.pallas import tpu as pltpu
 from jax.sharding import PartitionSpec as P
 
 HEAD_WIDTH = 128
+CHUNKS = 2
+PIECE = 16
+
+
+def remote(src, dst, send, recv, axis, index):
+    return pltpu.make_async_remote_copy(
+        src_ref=src,
+        dst_ref=dst,
+        send_sem=send,
+        recv_sem=recv,
+        device_id={axis: index},
+        device_id_type=pl.DeviceIdType.MESH,
+    )
+
+
+def mirror(a, s):
+    b = a
+    bit = 1
+    while bit < 4:
+        b = b + ((s // bit) % 2) * (bit - 2 * bit * ((a // bit) % 2))
+        bit *= 2
+    return b
+
+
+def attend_rows(q16, k_buf, v_buf, lens16, row0, kv_local, group, context):
+    qf = q16.astype(jnp.float32)
+    lane = lax.broadcasted_iota(jnp.int32, (8 * group, 2 * context), 1)
+    row = lax.broadcasted_iota(jnp.int32, (8 * group, 2 * context), 0) % 8
+    own_half = (lane // context) == (row % 2)
+    place = lane % context
+    pair = row // 2
+    out = [[None, None] for _ in range(kv_local * group)]
+    for half in range(2):
+        q8 = qf[half * 8 : half * 8 + 8]
+        lens = jnp.concatenate([lens16[half * 8 : half * 8 + 8]] * group, axis=0)
+        visible = own_half & (place < lens)
+        for g in range(kv_local):
+            lanes = slice(g * HEAD_WIDTH, (g + 1) * HEAD_WIDTH)
+            qs = jnp.concatenate(
+                [
+                    q8[:, (g * group + h) * HEAD_WIDTH : (g * group + h + 1) * HEAD_WIDTH]
+                    for h in range(group)
+                ],
+                axis=0,
+            ).astype(jnp.bfloat16)
+            keys = k_buf[pl.ds(row0 + half * 8, 8), :, lanes].reshape(8 * context, HEAD_WIDTH)
+            vals = v_buf[pl.ds(row0 + half * 8, 8), :, lanes].reshape(8 * context, HEAD_WIDTH)
+            cross = lax.dot_general(
+                qs, keys, (((1,), (1,)), ((), ())), preferred_element_type=jnp.float32
+            )
+            width = 2 * context
+            logits = cross[:, :width]
+            for j in range(1, 4):
+                logits = jnp.where(pair == j, cross[:, j * width : (j + 1) * width], logits)
+            logits = jnp.where(visible, logits * HEAD_WIDTH ** (-0.5), -1e30)
+            weights = jnp.exp(logits - jnp.max(logits, axis=1, keepdims=True))
+            probs = weights / jnp.sum(weights, axis=1, keepdims=True)
+            spread = jnp.concatenate(
+                [jnp.where(pair == j, probs, 0.0) for j in range(4)], axis=1
+            ).astype(jnp.bfloat16)
+            mixed = jnp.dot(spread, vals, preferred_element_type=jnp.float32)
+            for h in range(group):
+                out[g * group + h][half] = mixed[8 * h : 8 * h + 8]
+    return [jnp.concatenate(pair_of, axis=0).astype(jnp.bfloat16) for pair_of in out]
+
+
+def fused_kernel(
+    n,
+    tn,
+    q_ref,
+    k_hbm,
+    v_hbm,
+    len_ref,
+    radp_ref,
+    slot_ref,
+    w_hbm,
+    down_ref,
+    up_hbm,
+    out_ref,
+    k_buf,
+    v_buf,
+    w_buf,
+    gat,
+    part,
+    got,
+    base,
+    mids,
+    masks,
+    ups,
+    done,
+    kv_sem,
+    w_sem,
+    gs,
+    gr,
+    rs,
+    rr,
+    ms,
+    mr,
+    ks,
+    kr,
+    us,
+    ur,
+    xs,
+    xr,
+    ol,
+    os,
+    orr,
+):
+    a = lax.axis_index("adapter")
+    t = lax.axis_index("tensor")
+    rows, feat = q_ref.shape
+    cols = w_hbm.shape[1]
+    rank = down_ref.shape[2]
+    context = k_hbm.shape[1]
+    kv_local = k_hbm.shape[2] // HEAD_WIDTH
+    group = feat // (kv_local * HEAD_WIDTH)
+    quarter = rows // tn
+    share = rank // tn
+    steps = CHUNKS * n
+
+    for c in range(CHUNKS):
+        for x in range(tn):
+            at = pl.ds(x * quarter + c * PIECE, PIECE)
+            pltpu.make_async_copy(k_hbm.at[at], k_buf.at[at], kv_sem.at[0, c, x]).start()
+            pltpu.make_async_copy(v_hbm.at[at], v_buf.at[at], kv_sem.at[1, c, x]).start()
+    w_copy = pltpu.make_async_copy(w_hbm, w_buf, w_sem)
+    w_copy.start()
+    own_cols = pl.ds(pl.multiple_of(a * cols, 128), cols)
+    up_local = pltpu.make_async_copy(up_hbm.at[0, :, own_cols], ups.at[a], ol)
+    up_local.start()
+
+    barrier = pltpu.get_barrier_semaphore()
+    for d in range(1, n):
+        pl.semaphore_signal(
+            barrier, inc=1, device_id={"adapter": (a + d) % n}, device_id_type=pl.DeviceIdType.MESH
+        )
+    for d in range(1, tn):
+        pl.semaphore_signal(
+            barrier, inc=1, device_id={"tensor": (t + d) % tn}, device_id_type=pl.DeviceIdType.MESH
+        )
+    pl.semaphore_wait(barrier, n + tn - 2)
+
+    mine = pl.ds(pl.multiple_of(t * share, share), share)
+    up_sends = []
+    for d in range(1, n):
+        to = (a + d) % n
+        up_sends.append(
+            remote(
+                up_hbm.at[0, mine, pl.ds(pl.multiple_of(to * cols, 128), cols)],
+                ups.at[a, mine, :],
+                us.at[d - 1],
+                ur.at[a],
+                "adapter",
+                to,
+            )
+        )
+        up_sends[-1].start()
+    named = radp_ref[pl.ds(pl.multiple_of(t * quarter, quarter), quarter), :]
+    slot = jnp.zeros_like(named)
+    for k in range(n):
+        slot = slot + jnp.where(named == k, slot_ref[k], 0)
+    lane_slot = lax.broadcasted_iota(jnp.int32, (quarter, n * rank), 1) // rank
+    hot = jnp.where(lane_slot == slot, 1.0, 0.0).astype(jnp.bfloat16)
+    masks[a] = hot.reshape(CHUNKS, PIECE, n * rank)
+    mask_sends = []
+    for d in range(1, n):
+        to = (a + d) % n
+        mask_sends.append(
+            remote(masks.at[a], masks.at[a], ks.at[d - 1], kr.at[a], "adapter", to)
+        )
+        mask_sends[-1].start()
+
+    def up_line(b, c):
+        return remote(
+            gat.at[b, c], gat.at[b, c], gs.at[0, b, c], gr.at[b, c], "adapter", (a + 1) % n
+        )
+
+    def down_line(b, c):
+        return remote(
+            gat.at[b, c], gat.at[b, c], gs.at[1, b, c], gr.at[b, c], "adapter", (a + n - 1) % n
+        )
+
+    for c in range(CHUNKS):
+
+        def attend_step(x, carry, c=c):
+            row0 = pl.multiple_of(x * quarter + c * PIECE, PIECE)
+            at = pl.ds(row0, PIECE)
+            pltpu.make_async_copy(k_hbm.at[at], k_buf.at[at], kv_sem.at[0, c, x]).wait()
+            pltpu.make_async_copy(v_hbm.at[at], v_buf.at[at], kv_sem.at[1, c, x]).wait()
+            heads = attend_rows(
+                q_ref[at, :], k_buf, v_buf, len_ref[at, :], row0, kv_local, group, context
+            )
+            to = pl.ds(pl.multiple_of(x * PIECE, PIECE), PIECE)
+            for h, value in enumerate(heads):
+                gat[a, c, to, h * HEAD_WIDTH : (h + 1) * HEAD_WIDTH] = value
+            return carry
+
+        lax.fori_loop(0, tn, attend_step, 0)
+
+        @pl.when(a < n - 1)
+        def _(c=c):
+            up_line(a, c).start()
+
+        @pl.when(a > 0)
+        def _(c=c):
+            down_line(a, c).start()
+
+    share_sends = []
+    for d in range(1, n):
+        source = (a + d) % n
+        remote(ups.at[source, mine, :], ups.at[source, mine, :], us.at[0], ur.at[source],
+               "adapter", source).wait_recv()
+        for e in range(1, tn):
+            share_sends.append(
+                remote(
+                    ups.at[source, mine, :],
+                    ups.at[source, mine, :],
+                    xs.at[d - 1, e - 1],
+                    xr.at[d - 1, e - 1],
+                    "tensor",
+                    (t + e) % tn,
+                )
+            )
+            share_sends[-1].start()
+    w_copy.wait()
+
+    def scatter(i, e):
+        return remote(
+            part.at[i, (t + e) % tn], got.at[i, e - 1], rs.at[i, e - 1], rr.at[i, e - 1],
+            "tensor", (t + e) % tn,
+        )
+
+    def mid_send(c, b, i, d):
+        return remote(
+            mids.at[c, b, a], mids.at[c, b, a], ms.at[i, d - 1], mr.at[c, b, a],
+            "adapter", (a + d) % n,
+        )
+
+    def multiply(i):
+        c, s = i // n, i % n
+
+        @pl.when((s > 0) & (a - s >= 0))
+        def _():
+            up_line(a - s, c).wait_recv()
+
+            @pl.when(a < n - 1)
+            def _():
+                up_line(a - s, c).start()
+
+        @pl.when((s > 0) & (a + s < n))
+        def _():
+            down_line(a + s, c).wait_recv()
+
+            @pl.when(a > 0)
+            def _():
+                down_line(a + s, c).start()
+
+        b = mirror(a, s)
+        x = gat[b, c]
+        tile = 512
+        low = jnp.dot(x, down_ref[0], preferred_element_type=jnp.float32)
+        low = jnp.concatenate([low, jnp.zeros_like(low)], axis=1).astype(jnp.bfloat16)
+        part[i, :, :, cols : cols + 2 * rank] = low.reshape(tn, PIECE, 2 * rank)
+        for j in range(cols // tile):
+            y = jnp.dot(
+                x, w_buf[:, j * tile : (j + 1) * tile], preferred_element_type=jnp.float32
+            )
+            part[i, :, :, j * tile : (j + 1) * tile] = y.astype(jnp.bfloat16).reshape(
+                tn, PIECE, tile
+            )
+        for e in range(1, tn):
+            scatter(i, e).start()
+
+    def add_up(i):
+        c, s = i // n, i % n
+        b = mirror(a, s)
+        for e in range(1, tn):
+            scatter(i, e).wait_recv()
+        total = part[i, t].astype(jnp.float32)
+        for e in range(1, tn):
+            total = total + got[i, e - 1].astype(jnp.float32)
+        base[i] = total[:, :cols]
+        mids[c, b, a] = total[:, cols:].astype(jnp.bfloat16)
+        for d in range(1, n):
+            mid_send(c, b, i, d).start()
+
+    def result(c, s):
+        return remote(
+            done.at[c * n + s],
+            out_ref.at[pl.ds(pl.multiple_of(c * PIECE, PIECE), PIECE), own_cols],
+            os.at[c * n + s],
+            orr.at[c, a],
+            "adapter",
+            mirror(a, s),
+        )
+
+    def finish(c, s):
+        i = c * n + s
+        b = mirror(a, s)
+        for d in range(1, n):
+            source = (a + d) % n
+            remote(mids.at[c, b, source], mids.at[c, b, source], ms.at[0, 0],
+                   mr.at[c, b, source], "adapter", source).wait_recv()
+        low = jnp.concatenate(
+            [mids[c, b, k].astype(jnp.float32)[:, :rank] for k in range(n)], axis=1
+        )
+        low = jnp.where(masks[b, c].astype(jnp.float32) > 0.5, low, 0.0).astype(jnp.bfloat16)
+        delta = jnp.dot(
+            low, ups[...].reshape(n * rank, cols), preferred_element_type=jnp.float32
+        )
+        y = (base[i] + 2.0 * delta).astype(jnp.bfloat16)
+
+        @pl.when(s == 0)
+        def _():
+            out_ref[pl.ds(pl.multiple_of(c * PIECE, PIECE), PIECE), own_cols] = y
+
+        @pl.when(s > 0)
+        def _():
+            done[i] = y
+            result(c, s).start()
+
+    def step(i, carry):
+        @pl.when(i < steps)
+        def _():
+            multiply(i)
+
+        @pl.when(i > 0)
+        def _():
+            add_up(i - 1)
+
+        @pl.when(i == n)
+        def _():
+            up_local.wait()
+            for d in range(1, n):
+                source = (a + d) % n
+                remote(masks.at[source], masks.at[source], ks.at[0], kr.at[source],
+                       "adapter", source).wait_recv()
+                for e in range(1, tn):
+                    other = pl.ds(pl.multiple_of(((t + tn - e) % tn) * share, share), share)
+                    remote(ups.at[source, other, :], ups.at[source, other, :],
+                           xs.at[0, 0], xr.at[d - 1, e - 1],
+                           "tensor", (t + e) % tn).wait_recv()
+
+        @pl.when(i > n)
+        def _():
+            finish(0, i - n - 1)
+
+        return carry
+
+    lax.fori_loop(0, steps + 1, step, 0)
+
+    def last(s, carry):
+        finish(1, s)
+        return carry
+
+    lax.fori_loop(0, n, last, 0)
+
+    for c in range(CHUNKS):
+        for d in range(1, n):
+            source = (a + d) % n
+            there = pl.ds(pl.multiple_of(source * cols, 128), cols)
+            remote(done.at[0], out_ref.at[pl.ds(c * PIECE, PIECE), there], os.at[0],
+                   orr.at[c, source], "adapter", source).wait_recv()
+    for copy in up_sends + mask_sends + share_sends:
+        copy.wait_send()
+
+    def settle(i, carry):
+        c, s = i // n, i % n
+        b = mirror(a, s)
+        for e in range(1, tn):
+            scatter(i, e).wait_send()
+        for d in range(1, n):
+            mid_send(c, b, i, d).wait_send()
+
+        @pl.when(s > 0)
+        def _():
+            result(c, s).wait_send()
+
+        @pl.when((s <= a) & (a < n - 1))
+        def _():
+            up_line(s, c).wait_send()
+
+        @pl.when((s >= a) & (a > 0))
+        def _():
+            down_line(s, c).wait_send()
+
+        return carry
+
+    lax.fori_loop(0, steps, settle, 0)
+
+
+def fused(
+    queries,
+    cached_key_rows,
+    cached_value_rows,
+    cached_row_length,
+    row_adapter_index,
+    adapter_slot_index,
+    output_weight,
+    adapter_down_weight,
+    adapter_up_weight,
+):
+    n, tn = lax.axis_size("adapter"), lax.axis_size("tensor")
+    rows, feat = queries.shape
+    cols = output_weight.shape[1]
+    rank = adapter_down_weight.shape[2]
+    steps = CHUNKS * n
+    bf16, f32 = jnp.bfloat16, jnp.float32
+    dma = pltpu.SemaphoreType.DMA
+    vmem = pl.BlockSpec(memory_space=pltpu.VMEM)
+    hbm = pl.BlockSpec(memory_space=pl.ANY)
+    smem = pl.BlockSpec(memory_space=pltpu.SMEM)
+    return pl.pallas_call(
+        functools.partial(fused_kernel, n, tn),
+        out_shape=jax.ShapeDtypeStruct((rows // tn, n * cols), bf16),
+        in_specs=[vmem, hbm, hbm, vmem, vmem, smem, hbm, vmem, hbm],
+        out_specs=vmem,
+        scratch_shapes=[
+            pltpu.VMEM(cached_key_rows.shape, bf16),
+            pltpu.VMEM(cached_value_rows.shape, bf16),
+            pltpu.VMEM(output_weight.shape, bf16),
+            pltpu.VMEM((n, CHUNKS, tn * PIECE, feat), bf16),
+            pltpu.VMEM((steps, tn, PIECE, cols + 2 * rank), bf16),
+            pltpu.VMEM((steps, tn - 1, PIECE, cols + 2 * rank), bf16),
+            pltpu.VMEM((steps, PIECE, cols), f32),
+            pltpu.VMEM((CHUNKS, n, n, PIECE, 2 * rank), bf16),
+            pltpu.VMEM((n, CHUNKS, PIECE, n * rank), bf16),
+            pltpu.VMEM((n, rank, cols), bf16),
+            pltpu.VMEM((steps, PIECE, cols), bf16),
+            dma((2, CHUNKS, tn)),
+            dma,
+            dma((2, n, CHUNKS)),
+            dma((n, CHUNKS)),
+            dma((steps, tn - 1)),
+            dma((steps, tn - 1)),
+            dma((steps, n - 1)),
+            dma((CHUNKS, n, n)),
+            dma((n - 1,)),
+            dma((n,)),
+            dma((n - 1,)),
+            dma((n,)),
+            dma((n - 1, tn - 1)),
+            dma((n - 1, tn - 1)),
+            dma,
+            dma((steps,)),
+            dma((CHUNKS, n)),
+        ],
+        compiler_params=pltpu.CompilerParams(
+            collective_id=0, has_side_effects=True, vmem_limit_bytes=56 * 1024 * 1024
+        ),
+    )(
+        queries,
+        cached_key_rows,
+        cached_value_rows,
+        cached_row_length[:, None],
+        row_adapter_index,
+        adapter_slot_index,
+        output_weight,
+        adapter_down_weight,
+        adapter_up_weight,
+    )
 
 
 def per_device(
@@ -104,8 +569,9 @@
 
 
 def solution(mesh):
+    short_line = mesh.shape["adapter"] == 4 and mesh.shape["tensor"] == 4
     return jax.shard_map(
-        per_device,
+        fused if short_line else per_device,
         mesh=mesh,
         in_specs=(
             P(("group", "adapter"), "tensor"),

time: 257 us -> 82.4 us (0.32)
  waiting for transfers between devices: 181 us -> 0 us
  Pallas kernels: 0 us -> 75.6 us
  matrix products: 26.1 us -> 0 us
  between operations: 13.6 us -> 0.01 us
  blocking collectives: 12.3 us -> 0 us
  starting transfers between devices: 11.8 us -> 0 us
  local copies, waits for them, and re-layouts: 10.7 us -> 6.58 us
    unnamed x3 -> x0, waiting for transfers between devices: 77.5 us -> none
    pallas_call x0 -> x1, Pallas kernels: none -> 75.6 us  [fused(): pl.pallas_call(functools.partial(fused_kernel, n, tn), out_shape=jax.Shap...]
    all_to_all x3 -> x0, waiting for transfers between devices: 54.5 us -> none  [the longest x1 44.1 us: per_device(): lax.all_to_all(adapter_terms, 'adapter', split_axis=0, concat_axis=2, til...]
    all_gather x1 -> x0, waiting for transfers between devices: 48.6 us -> none  [per_device(): lax.all_gather(attended, 'adapter', axis=0, tiled=True)]
    dot_general x6 -> x0, matrix products: 21.4 us -> none  [the longest x1 10.5 us: per_device(): jnp.dot(lax.all_gather(attended, 'adapter', axis=0, tiled=True), output_w...]
    unnamed x1 -> x0, blocking collectives: 12.3 us -> none
    all_to_all x3 -> x0, starting transfers between devices: 11.7 us -> none  [the longest x1 4.6 us: per_device(): lax.all_to_all(shares.reshape(owner_count, quarter_rows, -1), 'adapter',...]
    sub x1 -> x0, matrix products: 4.71 us -> none  [per_device(): weights = jnp.exp(logits - highest)]
  transfers between devices with their start and end apart: 5 -> 0, of which waited for: 4 -> 0; matrix products, arithmetic and copies ran while one was open for 5% -> 0% of each run, Pallas kernels for 0% -> 0%
where the time goes in v1:
time: 82.4 us; the launch traced here: 82.2 us
  Pallas kernels  75.6 us (92%)
  local copies, waits for them, and re-layouts  6.58 us (8%)
    pallas_call x1, Pallas kernels, fused(): pl.pallas_call(functools.partial(fused_kernel, n, tn), out_shape=jax.Shap...  75.6 us
    unnamed x3, local copies, waits for them, and re-layouts  5.2 us

profile of v1, /device:TPU:0, one launch (start us, length us, event | category | flops | bytes accessed | tf_op | source)
XLA Modules:
  0.0 82.2 jit_solution(13571850144574512975)
XLA Ops:
  0.0 1.4 %copy.10.len_ref = s32[128,1]{1,0:T(8,128)} copy(s32[128,1]{0,1:T(1,128)} %bitcast.1) | data formatting | bytes 1024 | tf_op jit(solution)/shard_map/broadcast_in_dim | solution.py:465
  1.4 1.4 %copy.11.radp_ref = s32[128,1]{1,0:T(8,128)} copy(s32[128,1]{0,1:T(1,128)} %param.13) | data formatting | bytes 1024 | tf_op args[4]
  2.8 2.0 %copy.12.down_ref = bf16[1,2048,64]{2,1,0:T(8,128)(2,1)} copy(bf16[1,2048,64]{1,2,0:T(8,128)(2,1)} %param.16) | data formatting | bytes 524288 | tf_op args[7]
  4.7 75.6 %shard_map.91 = bf16[32,8192]{1,0:T(8,128)(2,1)} custom-call(bf16[128,2048]{1,0:T(8,128)(2,1)} %q_ref.1, bf16[128,64,256]{2,1,0:T(8,128)(2,1)} %k_hbm.1, bf16[128,64,256]{2,1,0:T(8,128)(2,1)} %v_hbm.1, s32[128,1]{1,0:T(8,128)} %copy.10.len_ref, s32[128,1]{1,0:T(8,128)} %copy.11.radp_ref, s32[4]{0:T(128)} %slot_ref.1, bf16[2048,2048]{1,0:T(8,128)(2,1)} %w_hbm.1, ...), custom_call_target="tpu_custom_call" | custom-call | tf_op jit(solution)/shard_map/pallas_call | solution.py:423
  80.3 1.9 %copy.14 = bf16[32,8192]{1,0:T(8,128)(2,1)} copy(bf16[32,8192]{1,0:T(8,128)(2,1)} %shard_map.91) | data formatting | bytes 1048576

commit v2 on v1

--- a/solution.py
+++ b/solution.py
@@ -30,6 +30,21 @@
         b = b + ((s // bit) % 2) * (bit - 2 * bit * ((a // bit) % 2))
         bit *= 2
     return b
+
+
+def as_columns(row):
+    count = row.shape[1]
+    own = lax.broadcasted_iota(jnp.int32, (count, count), 0) == lax.broadcasted_iota(
+        jnp.int32, (count, count), 1
+    )
+    line = jnp.where(own, jnp.broadcast_to(row.astype(jnp.float32), (count, count)), 0.0)
+    return jnp.broadcast_to(jnp.sum(line, axis=1, keepdims=True), (count, count))
+
+
+def step_bits(a, c, j):
+    left = 3 - j
+    inner = (a % 3 + 1) // 2
+    return (1 - c) * j + c * (left + inner * (left // 2 - 2 * (left // 3)))
 
 
 def attend_rows(q16, k_buf, v_buf, lens16, row0, kv_local, group, context):
@@ -43,7 +58,7 @@
     for half in range(2):
         q8 = qf[half * 8 : half * 8 + 8]
         lens = jnp.concatenate([lens16[half * 8 : half * 8 + 8]] * group, axis=0)
-        visible = own_half & (place < lens)
+        visible = own_half & (place.astype(jnp.float32) < lens)
         for g in range(kv_local):
             lanes = slice(g * HEAD_WIDTH, (g + 1) * HEAD_WIDTH)
             qs = jnp.concatenate(
@@ -90,10 +105,16 @@
     k_buf,
     v_buf,
     w_buf,
+    lens,
+    slots,
     gat,
     part,
     got,
+    half,
+    other,
     base,
+    lows,
+    low_got,
     mids,
     masks,
     ups,
@@ -104,6 +125,8 @@
     gr,
     rs,
     rr,
+    ls,
+    lr,
     ms,
     mr,
     ks,
@@ -118,9 +141,11 @@
 ):
     a = lax.axis_index("adapter")
     t = lax.axis_index("tensor")
+    core, chip = t % 2, t // 2
+    core_peer, chip_peer = mirror(t, 1), mirror(t, 2)
     rows, feat = q_ref.shape
     cols = w_hbm.shape[1]
-    rank = down_ref.shape[2]
+    rank = down_ref.shape[1]
     context = k_hbm.shape[1]
     kv_local = k_hbm.shape[2] // HEAD_WIDTH
     group = feat // (kv_local * HEAD_WIDTH)
@@ -165,12 +190,16 @@
             )
         )
         up_sends[-1].start()
-    named = radp_ref[pl.ds(pl.multiple_of(t * quarter, quarter), quarter), :]
+    lens[...] = as_columns(len_ref[...])
+    named = radp_ref[...]
     slot = jnp.zeros_like(named)
     for k in range(n):
         slot = slot + jnp.where(named == k, slot_ref[k], 0)
+    slots[...] = as_columns(slot)
+    slot = slots[pl.ds(pl.multiple_of(t * quarter, quarter), quarter), :]
+    slot = jnp.concatenate([slot] * (n * rank // rows), axis=1)
     lane_slot = lax.broadcasted_iota(jnp.int32, (quarter, n * rank), 1) // rank
-    hot = jnp.where(lane_slot == slot, 1.0, 0.0).astype(jnp.bfloat16)
+    hot = jnp.where(lane_slot.astype(jnp.float32) == slot, 1.0, 0.0).astype(jnp.bfloat16)
     masks[a] = hot.reshape(CHUNKS, PIECE, n * rank)
     mask_sends = []
     for d in range(1, n):
@@ -198,7 +227,7 @@
             pltpu.make_async_copy(k_hbm.at[at], k_buf.at[at], kv_sem.at[0, c, x]).wait()
             pltpu.make_async_copy(v_hbm.at[at], v_buf.at[at], kv_sem.at[1, c, x]).wait()
             heads = attend_rows(
-                q_ref[at, :], k_buf, v_buf, len_ref[at, :], row0, kv_local, group, context
+                q_ref[at, :], k_buf, v_buf, lens[at, :], row0, kv_local, group, context
             )
             to = pl.ds(pl.multiple_of(x * PIECE, PIECE), PIECE)
             for h, value in enumerate(heads):
@@ -207,109 +236,169 @@
 
         lax.fori_loop(0, tn, attend_step, 0)
 
-        @pl.when(a < n - 1)
-        def _(c=c):
-            up_line(a, c).start()
-
-        @pl.when(a > 0)
-        def _(c=c):
-            down_line(a, c).start()
-
-    share_sends = []
-    for d in range(1, n):
-        source = (a + d) % n
-        remote(ups.at[source, mine, :], ups.at[source, mine, :], us.at[0], ur.at[source],
-               "adapter", source).wait_recv()
-        for e in range(1, tn):
-            share_sends.append(
-                remote(
-                    ups.at[source, mine, :],
-                    ups.at[source, mine, :],
-                    xs.at[d - 1, e - 1],
-                    xr.at[d - 1, e - 1],
-                    "tensor",
-                    (t + e) % tn,
-                )
-            )
-            share_sends[-1].start()
-    w_copy.wait()
-
-    def scatter(i, e):
-        return remote(
-            part.at[i, (t + e) % tn], got.at[i, e - 1], rs.at[i, e - 1], rr.at[i, e - 1],
-            "tensor", (t + e) % tn,
-        )
-
-    def mid_send(c, b, i, d):
-        return remote(
-            mids.at[c, b, a], mids.at[c, b, a], ms.at[i, d - 1], mr.at[c, b, a],
-            "adapter", (a + d) % n,
-        )
-
-    def multiply(i):
-        c, s = i // n, i % n
-
-        @pl.when((s > 0) & (a - s >= 0))
-        def _():
-            up_line(a - s, c).wait_recv()
+        if c == 0:
 
             @pl.when(a < n - 1)
             def _():
-                up_line(a - s, c).start()
-
-        @pl.when((s > 0) & (a + s < n))
-        def _():
-            down_line(a + s, c).wait_recv()
+                up_line(a, 0).start()
 
             @pl.when(a > 0)
             def _():
-                down_line(a + s, c).start()
-
-        b = mirror(a, s)
-        x = gat[b, c]
+                down_line(a, 0).start()
+
+    w_copy.wait()
+
+    def part_of(index):
+        return pl.ds(pl.multiple_of(index * share, share), share)
+
+    def share_copy(d, k):
+        source = (a + d) % n
+        at = part_of(chip_peer if k == 2 else t)
+        return remote(
+            ups.at[source, at, :], ups.at[source, at, :], xs.at[d - 1, k], xr.at[d - 1, k],
+            "tensor", chip_peer if k == 1 else core_peer,
+        )
+
+    def share_wait(d, k):
+        source = (a + d) % n
+        at = part_of(mirror(t, k + 1))
+        remote(
+            ups.at[source, at, :], ups.at[source, at, :], xs.at[d - 1, k], xr.at[d - 1, k],
+            "tensor", chip_peer if k == 1 else core_peer,
+        ).wait_recv()
+
+    def low_send(c, b, e):
+        to = mirror(t, e)
+        return remote(
+            lows.at[c, b, to], low_got.at[c, b, e - 1], ls.at[c, b, e - 1], lr.at[c, b, e - 1],
+            "tensor", to,
+        )
+
+    def mid_send(c, b, d):
+        return remote(
+            mids.at[c, b, a], mids.at[c, b, a], ms.at[c, b, d - 1], mr.at[c, b, a],
+            "adapter", (a + d) % n,
+        )
+
+    def core_send(i):
+        return remote(
+            part.at[i, 1 - core], got.at[i], rs.at[i, 0], rr.at[i, 0], "tensor", core_peer
+        )
+
+    def chip_send(i):
+        return remote(half.at[i], other.at[i], rs.at[i, 1], rr.at[i, 1], "tensor", chip_peer)
+
+    def low(c, b):
+        y = lax.dot_general(
+            gat[b, c], down_ref[0], (((1,), (1,)), ((), ())), preferred_element_type=jnp.float32
+        )
+        y = jnp.concatenate([y, jnp.zeros_like(y)], axis=1).astype(jnp.bfloat16)
+        lows[c, b] = y.reshape(tn, PIECE, 2 * rank)
+        for e in range(1, tn):
+            low_send(c, b, e).start()
+
+    def mid(c, b):
+        total = lows[c, b, t].astype(jnp.float32)
+        for e in range(1, tn):
+            low_send(c, b, e).wait_recv()
+            total = total + low_got[c, b, e - 1].astype(jnp.float32)
+        mids[c, b, a] = total.astype(jnp.bfloat16)
+        for d in range(1, n):
+            mid_send(c, b, d).start()
+
+    def multiply(i):
+        c, j = i // n, i % n
+        below = (1 - c) * (a - j) + c * j
+        above = (1 - c) * (a + j) + c * (n - 1 - j)
+        from_below = (below >= 0) & (below < a)
+        from_above = (above < n) & (above > a)
+
+        @pl.when(from_above)
+        def _():
+            down_line(above, c).wait_recv()
+
+            @pl.when(a > 0)
+            def _():
+                down_line(above, c).start()
+
+        @pl.when((c == 1) & (above == a) & (a > 0))
+        def _():
+            down_line(a, 1).start()
+
+        @pl.when(from_below)
+        def _():
+            up_line(below, c).wait_recv()
+
+            @pl.when(a < n - 1)
+            def _():
+                up_line(below, c).start()
+
+        @pl.when((c == 1) & (below == a) & (a < n - 1))
+        def _():
+            up_line(a, 1).start()
+
+        @pl.when(from_above)
+        def _():
+            low(c, above)
+
+        @pl.when(from_below)
+        def _():
+            low(c, below)
+
+        @pl.when(j == 0)
+        def _():
+            low(c, a)
+
+        x = gat[mirror(a, step_bits(a, c, j)), c]
         tile = 512
-        low = jnp.dot(x, down_ref[0], preferred_element_type=jnp.float32)
-        low = jnp.concatenate([low, jnp.zeros_like(low)], axis=1).astype(jnp.bfloat16)
-        part[i, :, :, cols : cols + 2 * rank] = low.reshape(tn, PIECE, 2 * rank)
-        for j in range(cols // tile):
-            y = jnp.dot(
-                x, w_buf[:, j * tile : (j + 1) * tile], preferred_element_type=jnp.float32
-            )
-            part[i, :, :, j * tile : (j + 1) * tile] = y.astype(jnp.bfloat16).reshape(
-                tn, PIECE, tile
-            )
-        for e in range(1, tn):
-            scatter(i, e).start()
+        for k in range(cols // tile):
+            lanes = slice(k * tile, (k + 1) * tile)
+            y = jnp.dot(x, w_buf[:, lanes], preferred_element_type=jnp.float32)
+            y = y.astype(jnp.bfloat16)
+            for piece in range(tn):
+                part[i, piece % 2, piece // 2, :, lanes] = y[piece * PIECE : (piece + 1) * PIECE]
+        core_send(i).start()
+
+        @pl.when(from_above)
+        def _():
+            mid(c, above)
+
+        @pl.when(from_below)
+        def _():
+            mid(c, below)
+
+        @pl.when(j == 0)
+        def _():
+            mid(c, a)
+
+    def pair(i):
+        core_send(i).wait_recv()
+        away = part[i, core, 1 - chip].astype(jnp.float32) + got[i, 1 - chip].astype(jnp.float32)
+        half[i] = away.astype(jnp.bfloat16)
+        chip_send(i).start()
+        base[i] = part[i, core, chip].astype(jnp.float32) + got[i, chip].astype(jnp.float32)
 
     def add_up(i):
-        c, s = i // n, i % n
-        b = mirror(a, s)
-        for e in range(1, tn):
-            scatter(i, e).wait_recv()
-        total = part[i, t].astype(jnp.float32)
-        for e in range(1, tn):
-            total = total + got[i, e - 1].astype(jnp.float32)
-        base[i] = total[:, :cols]
-        mids[c, b, a] = total[:, cols:].astype(jnp.bfloat16)
-        for d in range(1, n):
-            mid_send(c, b, i, d).start()
-
-    def result(c, s):
+        chip_send(i).wait_recv()
+        base[i] = base[i] + other[i].astype(jnp.float32)
+
+    def result(c, j):
         return remote(
-            done.at[c * n + s],
+            done.at[c * n + j],
             out_ref.at[pl.ds(pl.multiple_of(c * PIECE, PIECE), PIECE), own_cols],
-            os.at[c * n + s],
+            os.at[c * n + j],
             orr.at[c, a],
             "adapter",
-            mirror(a, s),
-        )
-
-    def finish(c, s):
-        i = c * n + s
+            mirror(a, step_bits(a, c, j)),
+        )
+
+    def finish(c, j):
+        i = c * n + j
+        s = step_bits(a, c, j)
         b = mirror(a, s)
         for d in range(1, n):
             source = (a + d) % n
-            remote(mids.at[c, b, source], mids.at[c, b, source], ms.at[0, 0],
+            remote(mids.at[c, b, source], mids.at[c, b, source], ms.at[0, 0, 0],
                    mr.at[c, b, source], "adapter", source).wait_recv()
         low = jnp.concatenate(
             [mids[c, b, k].astype(jnp.float32)[:, :rank] for k in range(n)], axis=1
@@ -327,16 +416,35 @@
         @pl.when(s > 0)
         def _():
             done[i] = y
-            result(c, s).start()
+            result(c, j).start()
 
     def step(i, carry):
         @pl.when(i < steps)
         def _():
             multiply(i)
 
-        @pl.when(i > 0)
-        def _():
-            add_up(i - 1)
+        @pl.when(i == 1)
+        def _():
+            for d in range(1, n):
+                source = (a + d) % n
+                remote(ups.at[source, mine, :], ups.at[source, mine, :], us.at[0], ur.at[source],
+                       "adapter", source).wait_recv()
+                share_copy(d, 0).start()
+                share_copy(d, 1).start()
+
+        @pl.when(i == 2)
+        def _():
+            for d in range(1, n):
+                share_wait(d, 1)
+                share_copy(d, 2).start()
+
+        @pl.when((i > 0) & (i <= steps))
+        def _():
+            pair(i - 1)
+
+        @pl.when(i > 1)
+        def _():
+            add_up(i - 2)
 
         @pl.when(i == n)
         def _():
@@ -345,25 +453,24 @@
                 source = (a + d) % n
                 remote(masks.at[source], masks.at[source], ks.at[0], kr.at[source],
                        "adapter", source).wait_recv()
-                for e in range(1, tn):
-                    other = pl.ds(pl.multiple_of(((t + tn - e) % tn) * share, share), share)
-                    remote(ups.at[source, other, :], ups.at[source, other, :],
-                           xs.at[0, 0], xr.at[d - 1, e - 1],
-                           "tensor", (t + e) % tn).wait_recv()
-
-        @pl.when(i > n)
-        def _():
-            finish(0, i - n - 1)
+                share_wait(d, 0)
+                share_wait(d, 2)
+
+        @pl.when((i == n + 1) | (i == n + 2))
+        def _():
+            def early(k, inner):
+                finish(0, (i - n - 1) * 2 + k)
+                return inner
+
+            lax.fori_loop(0, 2, early, 0)
+
+        @pl.when(i >= n + 2)
+        def _():
+            finish(1, i - n - 2)
 
         return carry
 
-    lax.fori_loop(0, steps + 1, step, 0)
-
-    def last(s, carry):
-        finish(1, s)
-        return carry
-
-    lax.fori_loop(0, n, last, 0)
+    lax.fori_loop(0, steps + 2, step, 0)
 
     for c in range(CHUNKS):
         for d in range(1, n):
@@ -371,18 +478,22 @@
             there = pl.ds(pl.multiple_of(source * cols, 128), cols)
             remote(done.at[0], out_ref.at[pl.ds(c * PIECE, PIECE), there], os.at[0],
                    orr.at[c, source], "adapter", source).wait_recv()
-    for copy in up_sends + mask_sends + share_sends:
+    for copy in up_sends + mask_sends:
         copy.wait_send()
+    for d in range(1, n):
+        for k in range(3):
+            share_copy(d, k).wait_send()
 
     def settle(i, carry):
         c, s = i // n, i % n
-        b = mirror(a, s)
+        core_send(i).wait_send()
+        chip_send(i).wait_send()
         for e in range(1, tn):
-            scatter(i, e).wait_send()
+            low_send(c, s, e).wait_send()
         for d in range(1, n):
-            mid_send(c, b, i, d).wait_send()
-
-        @pl.when(s > 0)
+            mid_send(c, s, d).wait_send()
+
+        @pl.when(step_bits(a, c, s) > 0)
         def _():
             result(c, s).wait_send()
 
@@ -429,10 +540,16 @@
             pltpu.VMEM(cached_key_rows.shape, bf16),
             pltpu.VMEM(cached_value_rows.shape, bf16),
             pltpu.VMEM(output_weight.shape, bf16),
+            pltpu.VMEM((rows, rows), f32),
+            pltpu.VMEM((rows, rows), f32),
             pltpu.VMEM((n, CHUNKS, tn * PIECE, feat), bf16),
-            pltpu.VMEM((steps, tn, PIECE, cols + 2 * rank), bf16),
-            pltpu.VMEM((steps, tn - 1, PIECE, cols + 2 * rank), bf16),
+            pltpu.VMEM((steps, 2, tn // 2, PIECE, cols), bf16),
+            pltpu.VMEM((steps, tn // 2, PIECE, cols), bf16),
+            pltpu.VMEM((steps, PIECE, cols), bf16),
+            pltpu.VMEM((steps, PIECE, cols), bf16),
             pltpu.VMEM((steps, PIECE, cols), f32),
+            pltpu.VMEM((CHUNKS, n, tn, PIECE, 2 * rank), bf16),
+            pltpu.VMEM((CHUNKS, n, tn - 1, PIECE, 2 * rank), bf16),
             pltpu.VMEM((CHUNKS, n, n, PIECE, 2 * rank), bf16),
             pltpu.VMEM((n, CHUNKS, PIECE, n * rank), bf16),
             pltpu.VMEM((n, rank, cols), bf16),
@@ -441,9 +558,11 @@
             dma,
             dma((2, n, CHUNKS)),
             dma((n, CHUNKS)),
-            dma((steps, tn - 1)),
-            dma((steps, tn - 1)),
-            dma((steps, n - 1)),
+            dma((steps, 2)),
+            dma((steps, 2)),
+            dma((CHUNKS, n, tn - 1)),
+            dma((CHUNKS, n, tn - 1)),
+            dma((CHUNKS, n, n - 1)),
             dma((CHUNKS, n, n)),
             dma((n - 1,)),
             dma((n,)),
@@ -462,11 +581,11 @@
         queries,
         cached_key_rows,
         cached_value_rows,
-        cached_row_length[:, None],
-        row_adapter_index,
+        cached_row_length[None, :],
+        row_adapter_index.reshape(1, rows),
         adapter_slot_index,
         output_weight,
-        adapter_down_weight,
+        jnp.swapaxes(adapter_down_weight, 1, 2),
         adapter_up_weight,
     )
 

time: 82.4 us -> 127 us (1.54)
  Pallas kernels: 75.6 us -> 125 us
  local copies, waits for them, and re-layouts: 6.58 us -> 1.87 us
    pallas_call x1, Pallas kernels: 75.6 us -> 125 us  [fused(): pl.pallas_call(functools.partial(fused_kernel, n, tn), out_shape=jax.Shap...]
    unnamed x3 -> x1, local copies, waits for them, and re-layouts: 5.2 us -> 1.87 us
    broadcast_in_dim x1 -> x0, local copies, waits for them, and re-layouts: 1.38 us -> none  [fused(): cached_row_length[:, None]]
where the time goes in v2:
time: 127 us
  Pallas kernels  125 us (98%)
  local copies, waits for them, and re-layouts  1.87 us (1%)
    pallas_call x1, Pallas kernels, fused(): pl.pallas_call(functools.partial(fused_kernel, n, tn), out_shape=jax.Shap...  125 us

profile of v2, /device:TPU:0, one launch (start us, length us, event | category | flops | bytes accessed | tf_op | source)
XLA Modules:
  0.0 127.1 jit_solution(16322211280360902291)
XLA Ops:
  0.0 125.2 %shard_map.91 = bf16[32,8192]{1,0:T(8,128)(2,1)} custom-call(bf16[128,2048]{1,0:T(8,128)(2,1)} %q_ref.1, bf16[128,64,256]{2,1,0:T(8,128)(2,1)} %k_hbm.1, bf16[128,64,256]{2,1,0:T(8,128)(2,1)} %v_hbm.1, s32[1,128]{1,0:T(1,128)} %bitcast.4, s32[1,128]{1,0:T(1,128)} %bitcast.5, s32[4]{0:T(128)} %slot_ref.1, bf16[2048,2048]{1,0:T(8,128)(2,1)} %w_hbm.1, ...), custom_call_target="tpu_custom_call" | custom-call | tf_op jit(solution)/shard_map/pallas_call | solution.py:534
  125.2 1.9 %copy.11 = bf16[32,8192]{1,0:T(8,128)(2,1)} copy(bf16[32,8192]{1,0:T(8,128)(2,1)} %shard_map.91) | data formatting | bytes 1048576

commit v3 on v2

--- a/solution.py
+++ b/solution.py
@@ -39,12 +39,6 @@
     )
     line = jnp.where(own, jnp.broadcast_to(row.astype(jnp.float32), (count, count)), 0.0)
     return jnp.broadcast_to(jnp.sum(line, axis=1, keepdims=True), (count, count))
-
-
-def step_bits(a, c, j):
-    left = 3 - j
-    inner = (a % 3 + 1) // 2
-    return (1 - c) * j + c * (left + inner * (left // 2 - 2 * (left // 3)))
 
 
 def attend_rows(q16, k_buf, v_buf, lens16, row0, kv_local, group, context):
@@ -236,15 +230,13 @@
 
         lax.fori_loop(0, tn, attend_step, 0)
 
-        if c == 0:
-
-            @pl.when(a < n - 1)
-            def _():
-                up_line(a, 0).start()
-
-            @pl.when(a > 0)
-            def _():
-                down_line(a, 0).start()
+        @pl.when((a < n - 1) & (c * a == 0))
+        def _(c=c):
+            up_line(a, c).start()
+
+        @pl.when((a > 0) & (c * (n - 1 - a) == 0))
+        def _(c=c):
+            down_line(a, c).start()
 
     w_copy.wait()
 
@@ -308,8 +300,8 @@
 
     def multiply(i):
         c, j = i // n, i % n
-        below = (1 - c) * (a - j) + c * j
-        above = (1 - c) * (a + j) + c * (n - 1 - j)
+        below = a - j
+        above = a + j
         from_below = (below >= 0) & (below < a)
         from_above = (above < n) & (above > a)
 
@@ -321,10 +313,6 @@
             def _():
                 down_line(above, c).start()
 
-        @pl.when((c == 1) & (above == a) & (a > 0))
-        def _():
-            down_line(a, 1).start()
-
         @pl.when(from_below)
         def _():
             up_line(below, c).wait_recv()
@@ -333,9 +321,10 @@
             def _():
                 up_line(below, c).start()
 
-        @pl.when((c == 1) & (below == a) & (a < n - 1))
+        @pl.when((i == n - 2) & (a > 0) & (a < n - 1))
         def _():
             up_line(a, 1).start()
+            down_line(a, 1).start()
 
         @pl.when(from_above)
         def _():
@@ -349,7 +338,7 @@
         def _():
             low(c, a)
 
-        x = gat[mirror(a, step_bits(a, c, j)), c]
+        x = gat[mirror(a, j), c]
         tile = 512
         for k in range(cols // tile):
             lanes = slice(k * tile, (k + 1) * tile)
@@ -359,17 +348,20 @@
                 part[i, piece % 2, piece // 2, :, lanes] = y[piece * PIECE : (piece + 1) * PIECE]
         core_send(i).start()
 
-        @pl.when(from_above)
-        def _():
-            mid(c, above)
-
-        @pl.when(from_below)
-        def _():
-            mid(c, below)
+    def ranks(i):
+        c, j = i // n, i % n
 
         @pl.when(j == 0)
         def _():
             mid(c, a)
+
+        @pl.when((j > 0) & (a + j < n))
+        def _():
+            mid(c, a + j)
+
+        @pl.when((j > 0) & (a - j >= 0))
+        def _():
+            mid(c, a - j)
 
     def pair(i):
         core_send(i).wait_recv()
@@ -389,13 +381,12 @@
             os.at[c * n + j],
             orr.at[c, a],
             "adapter",
-            mirror(a, step_bits(a, c, j)),
+            mirror(a, j),
         )
 
     def finish(c, j):
         i = c * n + j
-        s = step_bits(a, c, j)
-        b = mirror(a, s)
+        b = mirror(a, j)
         for d in range(1, n):
             source = (a + d) % n
             remote(mids.at[c, b, source], mids.at[c, b, source], ms.at[0, 0, 0],
@@ -409,11 +400,11 @@
         )
         y = (base[i] + 2.0 * delta).astype(jnp.bfloat16)
 
-        @pl.when(s == 0)
+        @pl.when(j == 0)
         def _():
             out_ref[pl.ds(pl.multiple_of(c * PIECE, PIECE), PIECE), own_cols] = y
 
-        @pl.when(s > 0)
+        @pl.when(j > 0)
         def _():
             done[i] = y
             result(c, j).start()
@@ -432,7 +423,7 @@
                 share_copy(d, 0).start()
                 share_copy(d, 1).start()
 
-        @pl.when(i == 2)
+        @pl.when(i == 3)
         def _():
             for d in range(1, n):
                 share_wait(d, 1)
@@ -440,6 +431,7 @@
 
         @pl.when((i > 0) & (i <= steps))
         def _():
+            ranks(i - 1)
             pair(i - 1)
 
         @pl.when(i > 1)
@@ -456,21 +448,29 @@
                 share_wait(d, 0)
                 share_wait(d, 2)
 
-        @pl.when((i == n + 1) | (i == n + 2))
+        @pl.when((i == n + 2) | (i == n + 3))
         def _():
             def early(k, inner):
-                finish(0, (i - n - 1) * 2 + k)
+                finish(0, (i - n - 2) * 2 + k)
                 return inner
 
             lax.fori_loop(0, 2, early, 0)
 
-        @pl.when(i >= n + 2)
-        def _():
-            finish(1, i - n - 2)
-
         return carry
 
-    lax.fori_loop(0, steps + 2, step, 0)
+    lax.fori_loop(0, steps + 1, step, 0)
+
+    def last(k, carry):
+        late = k // 2
+
+        @pl.when(k == 2)
+        def _():
+            add_up(steps - 1)
+
+        finish(1, (1 - late) * (2 - k) + late * (9 - 3 * k))
+        return carry
+
+    lax.fori_loop(0, n, last, 0)
 
     for c in range(CHUNKS):
         for d in range(1, n):
@@ -493,7 +493,7 @@
         for d in range(1, n):
             mid_send(c, s, d).wait_send()
 
-        @pl.when(step_bits(a, c, s) > 0)
+        @pl.when(s > 0)
         def _():
             result(c, s).wait_send()
 

time: 127 us -> 72.3 us (0.57)
  Pallas kernels: 125 us -> 70.3 us
    pallas_call x1, Pallas kernels: 125 us -> 70.3 us  [fused(): pl.pallas_call(functools.partial(fused_kernel, n, tn), out_shape=jax.Shap...]
where the time goes in v3:
time: 72.3 us; the launch traced here: 72.2 us
  Pallas kernels  70.3 us (97%)
  local copies, waits for them, and re-layouts  1.87 us (3%)
    pallas_call x1, Pallas kernels, fused(): pl.pallas_call(functools.partial(fused_kernel, n, tn), out_shape=jax.Shap...  70.3 us
    unnamed x1, local copies, waits for them, and re-layouts  1.87 us

profile of v3, /device:TPU:0, one launch (start us, length us, event | category | flops | bytes accessed | tf_op | source)
XLA Modules:
  0.0 72.2 jit_solution(10517317755742764923)
XLA Ops:
  0.0 70.3 %shard_map.91 = bf16[32,8192]{1,0:T(8,128)(2,1)} custom-call(bf16[128,2048]{1,0:T(8,128)(2,1)} %q_ref.1, bf16[128,64,256]{2,1,0:T(8,128)(2,1)} %k_hbm.1, bf16[128,64,256]{2,1,0:T(8,128)(2,1)} %v_hbm.1, s32[1,128]{1,0:T(1,128)} %bitcast.4, s32[1,128]{1,0:T(1,128)} %bitcast.5, s32[4]{0:T(128)} %slot_ref.1, bf16[2048,2048]{1,0:T(8,128)(2,1)} %w_hbm.1, ...), custom_call_target="tpu_custom_call" | custom-call | tf_op jit(solution)/shard_map/pallas_call | solution.py:534
  70.3 1.9 %copy.11 = bf16[32,8192]{1,0:T(8,128)(2,1)} copy(bf16[32,8192]{1,0:T(8,128)(2,1)} %shard_map.91) | data formatting | bytes 1048576

commit v4 on v3

--- a/solution.py
+++ b/solution.py
@@ -321,7 +321,7 @@
             def _():
                 up_line(below, c).start()
 
-        @pl.when((i == n - 2) & (a > 0) & (a < n - 1))
+        @pl.when((i == n - 3) & (a > 0) & (a < n - 1))
         def _():
             up_line(a, 1).start()
             down_line(a, 1).start()

time: 72.3 us -> 70.8 us (0.979)
  Pallas kernels: 70.3 us -> 68.8 us
    pallas_call x1, Pallas kernels: 70.3 us -> 68.8 us  [fused(): pl.pallas_call(functools.partial(fused_kernel, n, tn), out_shape=jax.Shap...]
where the time goes in v4:
time: 70.8 us; the launch traced here: 70.7 us
  Pallas kernels  68.8 us (97%)
  local copies, waits for them, and re-layouts  1.87 us (3%)
    pallas_call x1, Pallas kernels, fused(): pl.pallas_call(functools.partial(fused_kernel, n, tn), out_shape=jax.Shap...  68.8 us
    unnamed x1, local copies, waits for them, and re-layouts  1.87 us

profile of v4, /device:TPU:0, one launch (start us, length us, event | category | flops | bytes accessed | tf_op | source)
XLA Modules:
  0.0 70.7 jit_solution(592642726076229903)
XLA Ops:
  0.0 68.8 %shard_map.91 = bf16[32,8192]{1,0:T(8,128)(2,1)} custom-call(bf16[128,2048]{1,0:T(8,128)(2,1)} %q_ref.1, bf16[128,64,256]{2,1,0:T(8,128)(2,1)} %k_hbm.1, bf16[128,64,256]{2,1,0:T(8,128)(2,1)} %v_hbm.1, s32[1,128]{1,0:T(1,128)} %bitcast.4, s32[1,128]{1,0:T(1,128)} %bitcast.5, s32[4]{0:T(128)} %slot_ref.1, bf16[2048,2048]{1,0:T(8,128)(2,1)} %w_hbm.1, ...), custom_call_target="tpu_custom_call" | custom-call | tf_op jit(solution)/shard_map/pallas_call | solution.py:534
  68.8 1.9 %copy.11 = bf16[32,8192]{1,0:T(8,128)(2,1)} copy(bf16[32,8192]{1,0:T(8,128)(2,1)} %shard_map.91) | data formatting | bytes 1048576
